TPU v7x, 256 devices: a whole 4x4x8 slice. The times are simulated.
256 devices in a mesh: rep: 16 (over z_hi, x), shard: 16 (over y, z_lo, core).
Axes of the slice: x: 4, y: 4, z: 8 (z_hi: 4, z_lo: 2; z = z_hi * 2 + z_lo), core: 2. Of those that a mesh axis runs over, the one named last changes fastest.
Arguments:
- inputs: bfloat16 [131072, 4608], P(('rep', 'shard')), may hold values from -6 to 6
- gain: bfloat16 [4608], P('shard'), may hold values from -0.5 to 0.5
- weight: bfloat16 [4608, 1024], P('shard'), may hold values from -0.09375 to 0.09375
- upstream: bfloat16 [131072, 1024], P(('rep', 'shard')), may hold values from -6 to 6
Outputs:
- input_grad: bfloat16 [131072, 4608], P(('rep', 'shard'))
- weight_grad: float32 [4608, 1024], P('shard')
- gain_grad: float32 [4608], P('shard')
All inputs are finite; a program needn't handle non-finite values.
Results may differ from a plain program's by a relative error of at most 0.0028.
Values may be sent and summed in bfloat16 or wider, within the bound.
A program may use at most 128 MiB of HBM per device.

v0:
```python
import math

import jax
import jax.numpy as jnp
from jax import lax
from jax.sharding import PartitionSpec as P


def local(inputs, gain, weight, upstream):
    n_rep = lax.axis_size("rep")
    n_shard = lax.axis_size("shard")
    own_rows = gain.shape[0]
    tokens_here = inputs.shape[0]
    factor = 1.0 / math.sqrt(tokens_here * n_rep * n_shard)
    weight_piece = lax.all_gather(weight, "shard", axis=0, tiled=True)
    gain_piece = lax.all_gather(gain, "shard", axis=0, tiled=True)
    product = lax.dot_general(
        upstream, weight_piece, (((1,), (1,)), ((), ())), preferred_element_type=jnp.float32
    )
    delta = product
    gain_full = gain_piece
    delta, gain_full = (delta, gain_full)
    scale_gain = 1.0 + gain_full.astype(jnp.float32)
    floats = inputs.astype(jnp.float32)
    inverse = lax.rsqrt(jnp.mean(floats * floats, axis=-1, keepdims=True) + 1e-06)
    normed = floats * inverse
    hidden = (normed * scale_gain).astype(jnp.bfloat16)
    scaled = delta * scale_gain
    input_grad = (
        inverse * (scaled - normed * jnp.mean(scaled * normed, axis=-1, keepdims=True))
    ).astype(jnp.bfloat16)
    gain_part = jnp.sum(delta * normed, axis=0)
    shard_grad = lax.psum_scatter(
        lax.dot_general(
            hidden, upstream, (((0,), (0,)), ((), ())), preferred_element_type=jnp.float32
        ),
        "shard",
        scatter_dimension=0,
        tiled=True,
    )
    weight_grad = lax.psum(shard_grad, "rep") * factor
    gain_total = lax.psum(gain_part, ("rep", "shard"))
    gain_grad = (
        lax.dynamic_slice_in_dim(gain_total, lax.axis_index("shard") * own_rows, own_rows, 0)
        * factor
    )
    return (input_grad, weight_grad, gain_grad)


def solution(mesh):
    return jax.shard_map(
        local,
        mesh=mesh,
        in_specs=(
            P(("rep", "shard"), None),
            P("shard"),
            P("shard", None),
            P(("rep", "shard"), None),
        ),
        out_specs=(P(("rep", "shard"), None), P("shard", None), P("shard")),
        check_vma=False,
    )
```

profile of v0, /device:TPU:8, one launch (start us, length us, event | category | flops | bytes accessed | tf_op | source)
XLA Modules:
  0.0 470.9 jit_solution(7672571676459108393)
XLA Ops:
  7.2 0.0 copy-start
  7.2 0.0 all-gather.2.cloned.1.call-start
  7.2 0.7 all-gather.2.cloned.1.call-update
  7.9 0.0 reduce-scatter.2.cloned.1.call-start
  8.0 1.3 dynamic-slice
  9.9 0.9 dynamic-update-slice
  10.8 50.3 %all-reduce = bf16[4608]{0:T(1024)(128)(2,1)S(1)} all-reduce(bf16[4608]{0:T(1024)(128)(2,1)S(1)} %dynamic-update-slice), channel_id=1, replica_groups=mesh['rep'=16,'shard'=16] {'shard'}, use_global_device_ids=true, to_apply=%add | all-reduce | flops 4608 | bytes 18432
  61.1 3.4 fusion.10
  64.6 0.0 copy-done
  64.6 11.7 %fusion.11 = f32[4608,1024]{1,0:T(8,128)} fusion(bf16[512,1024]{1,0:T(8,128)(2,1)S(1)} %copy-done, bf16[512,4608]{1,0:T(8,128)(2,1)} %param.4, f32[4608]{0:T(1024)S(1)} %convert_add_fusion, f32[512]{0:T(512)S(1)} %add_rsqrt_fusion), kind=kOutput, calls=%fused_computation.13 | convolution fusion | flops 4841275392 | bytes 24662016 | tf_op jit(solution)/shard_map/dot_general | solution.py:34
  76.3 0.0 reduce-scatter.2.cloned.1.call-update
  76.3 0.0 all-reduce.3.cloned.1.call-start
  76.4 0.0 all-gather.2.cloned.1.call-done
  76.4 13.1 %fusion.9 = (f32[4608]{0:T(1024)S(1)}, f32[512]{0:T(512)S(1)}, f32[512,4608]{1,0:T(8,128)}) fusion(bf16[512,4608]{1,0:T(8,128)(2,1)} %param.4, f32[512]{0:T(512)S(1)} %add_rsqrt_fusion, f32[4608]{0:T(1024)S(1)} %convert_add_fusion, bf16[512,1024]{1,0:T(8,128)(2,1)S(1)} %copy-done, bf16[4608,1024]{1,0:T(8,128)(2,1)} %all-gather.2.cloned.1.call-done), kind=kOutput, calls=%fused_computation.11 | convolution fusion | flops 4848348160 | bytes 24682496 | tf_op jit(solution)/shard_map/dot_general | solution.py:17
  89.5 83.2 %psum.15 = f32[4608]{0:T(1024)S(1)} all-reduce(f32[4608]{0:T(1024)S(1)} %get-tuple-element.3), channel_id=1, replica_groups=mesh['rep'=16,'shard'=16] {'rep','shard'}, use_global_device_ids=true, to_apply=%region_5.0 | all-reduce | flops 4608 | bytes 36864 | tf_op jit(solution)/shard_map/psum | solution.py:42
  172.7 0.7 dynamic-slice_multiply_fusion
  173.4 114.2 %reduce-scatter.2.cloned.1.call-done = f32[288,1024]{1,0:T(8,128)} async-done(((f32[4608,1024]{1,0:T(8,128)}), f32[288,1024]{1,0:T(8,128)}) %reduce-scatter.2.cloned.1.call-update) | async-done | bytes 1179664 | tf_op jit(solution)/shard_map/reduce_scatter | solution.py:33
  287.5 0.0 all-reduce.3.cloned.1.call-update
  287.6 10.3 %fusion.7 = bf16[512,4608]{1,0:T(8,128)(2,1)} fusion(bf16[512,4608]{1,0:T(8,128)(2,1)} %param.4, f32[512,4608]{1,0:T(8,128)} %get-tuple-element.5, f32[512]{0:T(512)S(1)} %broadcast_multiply_fusion.1, f32[4608]{0:T(1024)S(1)} %convert_add_fusion, f32[512]{0:T(512)S(1)} %add_rsqrt_fusion), kind=kLoop, calls=%fused_computation.9 | loop fusion | flops 16515072 | bytes 18896896 | tf_op jit(solution)/shard_map/convert_element_type | solution.py:31
  297.8 164.1 %all-reduce.3.cloned.1.call-done = f32[288,1024]{1,0:T(8,128)} async-done(((f32[288,1024]{1,0:T(8,128)}), f32[288,1024]{1,0:T(8,128)}) %all-reduce.3.cloned.1.call-update) | async-done | bytes 1179664 | tf_op jit(solution)/shard_map/psum | solution.py:41
  461.9 2.5 broadcast_multiply_fusion
  (4 shorter events, 0.0 us)
Async XLA Ops:
  7.2 57.4 %copy-start = (bf16[512,1024]{1,0:T(8,128)(2,1)S(1)}, bf16[512,1024]{1,0:T(8,128)(2,1)}, u32[]{:S(2)}) copy-start(bf16[512,1024]{1,0:T(8,128)(2,1)} %param.7) | copy-start | bytes 3145732
  7.2 69.2 %all-gather.2.cloned.1.call-start = ((), (), s32[]{:S(2)}) async-start(), calls=%async_computation.1 | async-start | bytes 10027008 | tf_op jit(solution)/shard_map/all_gather | solution.py:15
  7.9 279.6 %reduce-scatter.2.cloned.1.call-start = ((), (), s32[]{:S(2)}) async-start(), calls=%async_computation.2 | async-start | bytes 20054016 | tf_op jit(solution)/shard_map/reduce_scatter | solution.py:33
  76.3 385.6 %all-reduce.3.cloned.1.call-start = ((), (), s32[]{:S(2)}) async-start(), calls=%async_computation.3 | async-start | bytes 2359296 | tf_op jit(solution)/shard_map/psum | solution.py:41
Sparse Core Ops, SparseCore 0:
  9.9 62.3 all-gather.1
  76.4 211.0 reduce-scatter.1
  290.2 171.6 all-reduce.2
where the time goes:
time: 471 us
  waiting for transfers between devices  279 us (59%)
  blocking collectives  134 us (28%)
  matrix products  24.8 us (5%)
  other arithmetic  16.8 us (4%)
  between operations  14.5 us (3%)
    psum x1, waiting for transfers between devices, local(): weight_grad = lax.psum(shard_grad, 'rep') * factor  164 us
    reduce_scatter x1, waiting for transfers between devices, local(): lax.psum_scatter(lax.dot_general(hidden, upstream, (((0,), (0,)), ((), ()...  114 us
    psum x1, blocking collectives, local(): gain_total = lax.psum(gain_part, ('rep', 'shard'))  83.2 us
    unnamed x1, blocking collectives  50.3 us
    dot_general x1, matrix products, local(): lax.dot_general(upstream, weight_piece, (((1,), (1,)), ((), ())), preferr...  13.1 us
    dot_general x1, matrix products, local(): lax.dot_general(hidden, upstream, (((0,), (0,)), ((), ())), preferred_ele...  11.7 us
    convert_element_type x1, other arithmetic, local(): input_grad = (inverse * (scaled - normed * jnp.mean(scaled * normed, axis...  10.3 us
  transfers between devices with their start and end apart: 3, of which 2 were waited for; matrix products, arithmetic and copies ran while one was open for 9% of the time, Pallas kernels for 0%

commit v1 on v0

v1 whole, which is shorter than its diff:
```python
import math

import jax
import jax.numpy as jnp
from jax import lax
from jax.experimental import pallas as pl
from jax.experimental.pallas import tpu as pltpu
from jax.sharding import PartitionSpec as P

MESH = pl.DeviceIdType.MESH
F32 = jnp.float32
BF16 = jnp.bfloat16
TOK = 512
D = 4608
COLS = 1024
ROWS = 288
HALF = D // 2
SUB = 384
QUART = COLS // 4
PAD = D + 128
STRIP = 48
CHUNK = 4 * STRIP
CHUNKS = HALF // CHUNK
STRIPS = ROWS // STRIP
HOLD = 5
FACTOR = 1.0 / math.sqrt(131072)


def ds(start, size, unit):
    return pl.ds(pl.multiple_of(start, unit), size)


def remote(src, dst, send, recv, device):
    return pltpu.make_async_remote_copy(
        src_ref=src, dst_ref=dst, send_sem=send, recv_sem=recv, device_id=device, device_id_type=MESH
    )


def each(first, last, step):
    def body(t, carry):
        step(t)
        return carry

    lax.fori_loop(first, last, body, 0)


def kernel(
    x_hbm, gain, w_hbm, u_hbm,
    ig, wg, gg,
    xv, wv, sv, ht, hs, ups, inv, rd, gfull, gsum, gbuf, gone, gtwo, gmine, win,
    part, s1, l1, r1, s2, l2, r2, s3, r3, zs, zr, fb, ar,
    ld_x, ld_u, ld_w,
    gb_s, gb_r, g1_s, g1_r, g2_s, g2_r,
    u_s, u_r, h_s, h_r,
    wy_s, wy_r, wz_s, wz_r, wc_s, wc_r,
    s1_s, s1_r, s2_s, s2_r, s3_s, s3_r, z_s, z_r, a_s, a_r, b_s, b_r,
):
    rep = lax.axis_index("rep")
    me = lax.axis_index("shard")
    x, zhi = rep % 4, rep // 4
    y, zlo, c = me // 4, (me // 2) % 2, me % 2
    z = zhi * 2 + zlo

    def dev(xx, yy, zz, cc):
        return ((zz // 2) * 4 + xx, (yy * 2 + zz % 2) * 2 + cc)

    sib = (rep, me + 1 - 2 * c)
    right, left = dev((x + 1) % 4, y, z, c), dev((x + 3) % 4, y, z, c)
    up, down = dev(x, y, (z + 1) % 8, c), dev(x, y, (z + 7) % 8, c)

    row = jnp.concatenate([gain[...].astype(F32).reshape(1, ROWS), jnp.zeros((1, 512 - ROWS), F32)], axis=1)
    win[...] = pltpu.roll(jnp.broadcast_to(row, (8, 512)), (32 * me) % 128, 1)[:1]

    def load_x(k):
        rows = ds(k * 64, 64, 64)
        return pltpu.make_async_copy(x_hbm.at[rows, :], xv.at[rows, :], ld_x.at[k])

    each(0, 8, lambda k: load_x(k).start())
    own_tok = ds(c * TOK, TOK, TOK)
    load_u = pltpu.make_async_copy(u_hbm, ups.at[own_tok, :], ld_u)
    load_u.start()
    own_rows = ds(me * ROWS, ROWS, 32)
    load_w = pltpu.make_async_copy(w_hbm, wv.at[own_rows, :], ld_w)
    load_w.start()

    barrier = pltpu.get_barrier_semaphore()

    def hello(device):
        pl.semaphore_signal(barrier, inc=1, device_id=device, device_id_type=MESH)

    each(1, 16, lambda t: hello((rep, (me + t) % 16)))
    each(1, 16, lambda t: hello(((rep + t) % 16, me)))
    each(1, 4, lambda t: hello((((zhi + t) % 4) * 4 + x, (y * 2 + 1 - zlo) * 2 + c)))
    def norm_block(k):
        load_x(k).wait()
        rows = ds(k * 64, 64, 64)
        total = jnp.zeros((64, 128), F32)
        for j in range(D // 512):
            v = xv[rows, j * 512:(j + 1) * 512].astype(F32)
            v = v * v
            total = total + ((v[:, :128] + v[:, 128:256]) + (v[:, 256:384] + v[:, 384:]))
        mean = jnp.sum(total, axis=-1, keepdims=True) * (1.0 / D)
        inv[rows, :] = jnp.broadcast_to(lax.rsqrt(mean + 1e-06), (64, 128))

    each(0, 8, norm_block)

    pl.semaphore_wait(barrier, 33)

    def gain_copy(t):
        return remote(win, gbuf.at[me], gb_s.at[t], gb_r.at[t], (rep, (me + t) % 16))

    each(1, 16, lambda t: gain_copy(t).start())
    gbuf[me] = win[...]
    u_copy = remote(u_hbm, ups.at[own_tok, :], u_s, u_r, sib)
    u_copy.start()

    def w_half(d, zl, cc, h):
        return ds(((((y + d) % 4) * 2 + zl) * 2 + cc) * ROWS + h * 144, 144, 16)

    def y_own(way, h):
        rows = w_half(0, zlo, c, h)
        to = dev(x, (y + (1 if way == 0 else 3)) % 4, z, c)
        return remote(wv.at[rows, :], wv.at[rows, :], wy_s.at[way, h], wy_r.at[way, h], to)

    def y_pass(way):
        rows = w_half(3 if way == 0 else 1, zlo, c, way)
        to = dev(x, (y + (1 if way == 0 else 3)) % 4, z, c)
        return remote(wv.at[rows, :], wv.at[rows, :], wy_s.at[2, way], wy_r.at[2, way], to)

    def z_half(d, h):
        rows = w_half(d, zlo, c, h)
        return remote(wv.at[rows, :], wv.at[rows, :], wz_s.at[d, h], wz_r.at[d, h], up if h == 0 else down)

    def c_half(d, h, k):
        rows = w_half(d, zlo if k == 0 else 1 - zlo, c, h)
        return remote(wv.at[rows, :], wv.at[rows, :], wc_s.at[d, h, k], wc_r.at[d, h, k], sib)

    def arrive(rows, sem):
        remote(wv.at[rows, :], wv.at[rows, :], wc_s.at[0, 0, 0], sem, sib).wait_recv()

    def w_have(d, h):
        z_half(d, h).start()
        c_half(d, h, 0).start()

    def w_near(h, k):
        way = h if k == 0 else 1 - h
        d = 3 if way == 0 else 1
        arrive(w_half(d, zlo, c, h), wy_r.at[way, h])
        if k == 0:
            y_pass(way).start()
        w_have(d, h)

    def w_far(h):
        arrive(w_half(2, zlo, c, h), wy_r.at[2, h])
        w_have(2, h)

    def w_other(d, h):
        arrive(w_half(d, 1 - zlo, c, h), wz_r.at[d, h])
        c_half(d, h, 1).start()

    load_w.wait()
    for way in (0, 1):
        y_own(way, way).start()
        w_have(0, way)
    for way in (0, 1):
        y_own(way, 1 - way).start()

    def gain_wait(t):
        remote(win, gbuf.at[(me + 16 - t) % 16], gb_s.at[t], gb_r.at[t], sib).wait_recv()

    each(1, 16, gain_wait)
    gfull[...] = jnp.ones((1, PAD), F32)
    for s in range(16):
        at = (ROWS * s) // 128 * 128
        gfull[:, at:at + 512] = gfull[:, at:at + 512] + gbuf[s]

    def inv3(rows):
        iv = inv[rows, :]
        return jnp.concatenate([iv, iv, iv], axis=1)

    def hidden_block(j, at_feature, out, at_lane):
        feats = ds(at_feature + j * SUB, SUB, 128)
        scale = gfull[:, feats]

        def tokens(k):
            rows = ds(k * 128, 128, 128)
            v = xv[rows, feats].astype(F32) * inv3(rows)
            v = (v * scale).astype(BF16).T
            for e in range(SUB // STRIP):
                strip = j * (SUB // STRIP) + e
                shard, nth = strip // STRIPS, strip % STRIPS
                to = ((shard // 4) * STRIPS + nth) * CHUNK + ((shard % 2) * 2 + (shard // 2) % 2) * STRIP
                out[ds(to, STRIP, 16), ds(at_lane + k * 128, 128, 128)] = v[e * STRIP:(e + 1) * STRIP]

        each(0, 4, tokens)

    def h_copy(j):
        rows = ds(j * CHUNK, CHUNK, CHUNK)
        return remote(hs.at[rows, :], ht.at[rows, own_tok], h_s.at[j], h_r.at[j], sib)

    def h_wait(j):
        rows = ds(j * CHUNK, CHUNK, CHUNK)
        remote(hs.at[rows, :], ht.at[rows, ds((1 - c) * TOK, TOK, TOK)], h_s.at[j], h_r.at[j], sib).wait_recv()

    def hidden_other(j):
        hidden_block(j, (1 - c) * HALF, hs, 0)

    def hidden_own(j):
        hidden_block(j, c * HALF, ht, c * TOK)

    each(0, 3, hidden_other)
    each(0, STRIPS, lambda j: h_copy(j).start())
    each(0, 3, hidden_own)
    load_u.wait()
    remote(u_hbm, ups.at[ds((1 - c) * TOK, TOK, TOK), :], u_s, u_r, sib).wait_recv()

    rd[...] = jnp.zeros_like(rd)
    gsum[...] = jnp.zeros_like(gsum)

    def delta(d):
        for h in range(2):
            for k in range(2):
                arrive(w_half(d, zlo if k == 0 else 1 - zlo, 1 - c, h), wc_r.at[d, h, k])

        def block(j):
            at = ((y + d) % 4) * 1152 + j * SUB
            feats = ds(at, SUB, 128)
            sv[:, feats] = lax.dot_general(
                ups[own_tok, :], wv[ds(at, SUB, 32), :], (((1,), (1,)), ((), ())), preferred_element_type=F32
            )
            scale = gfull[:, feats]

            def tokens(k, col):
                rows = ds(k * 64, 64, 64)
                dl = sv[rows, feats]
                nm = xv[rows, feats].astype(F32) * inv3(rows)
                dn = dl * nm
                sn = dn * scale
                sv[rows, feats] = dl * scale
                rd[rows, :] = rd[rows, :] + (sn[:, :128] + sn[:, 128:256] + sn[:, 256:])
                return col + jnp.sum(dn.reshape(8, 8, SUB), axis=0)

            col = lax.fori_loop(0, 8, tokens, jnp.zeros((8, SUB), F32))
            gsum[:, feats] = jnp.sum(col, axis=0, keepdims=True)

        each(0, 3, block)

    def finish():
        def mean(k):
            rows = ds(k * 64, 64, 64)
            m = jnp.sum(rd[rows, :], axis=-1, keepdims=True) * (1.0 / D)
            rd[rows, :] = jnp.broadcast_to(m, (64, 128))

        each(0, 8, mean)

        def block(j):
            rows = ds(j * 64, 64, 64)

            def part_of(k):
                feats = ds(k * SUB, SUB, 128)
                iv = inv3(rows)
                m = rd[rows, :]
                nm = xv[rows, feats].astype(F32) * iv
                ig[rows, feats] = (iv * (sv[rows, feats] - nm * jnp.concatenate([m, m, m], axis=1))).astype(BF16)

            each(0, 12, part_of)

        each(0, 8, block)

    def gain_window(s):
        return ds(s * ROWS - (32 * s) % 128, 512, 128)

    def g1_copy(t):
        to = (me + t) % 16
        return remote(gsum.at[:, gain_window(to)], gone.at[me], g1_s.at[t], g1_r.at[t], (rep, to))

    def g1_wait(t):
        remote(gmine, gone.at[(me + 16 - t) % 16], g1_s.at[t], g1_r.at[t], sib).wait_recv()

    def g2_copy(t):
        return remote(gmine, gtwo.at[rep], g2_s.at[t], g2_r.at[t], ((rep + t) % 16, me))

    def g2_wait(t):
        remote(gmine, gtwo.at[(rep + 16 - t) % 16], g2_s.at[t], g2_r.at[t], sib).wait_recv()

    def gain_first():
        each(1, 16, lambda t: g1_copy(t).start())
        gone[me] = gsum[:, gain_window(me)]

    def gain_second():
        each(1, 16, g1_wait)
        total = gone[0]
        for s in range(1, 16):
            total = total + gone[s]
        gmine[...] = total
        gtwo[rep] = total
        each(1, 16, lambda t: g2_copy(t).start())

    def gain_third():
        each(1, 16, g2_wait)
        total = gtwo[0]
        for s in range(1, 16):
            total = total + gtwo[s]
        total = jnp.broadcast_to(total * FACTOR, (8, 512))
        gg[...] = pltpu.roll(total, (512 - (32 * me) % 128) % 512, 1)[0, :ROWS]

    def s1_copy(j, h):
        return remote(s1.at[j, h], (l1 if h == 0 else r1).at[j], s1_s.at[j, h], s1_r.at[j, h], right if h == 0 else left)

    def s1_wait(j, h):
        remote(s1.at[j, h], (l1 if h == 0 else r1).at[j], s1_s.at[j, h], s1_r.at[j, h], left).wait_recv()

    def s2_copy(j, h):
        return remote(s2.at[j, h], (l2 if h == 0 else r2).at[j], s2_s.at[j, h], s2_r.at[j, h], right if h == 0 else left)

    def s2_wait(j, h):
        remote(s2.at[j, h], (l2 if h == 0 else r2).at[j], s2_s.at[j, h], s2_r.at[j, h], left).wait_recv()

    def matmul(j):
        h_wait(j)
        slot = j % HOLD
        rows = ds(j * CHUNK, CHUNK, CHUNK)

        def quarter(q):
            return jnp.dot(ht[rows, :], ups[:, ds(q * QUART, QUART, 128)], preferred_element_type=F32)

        far = quarter((x + 2) % 4).astype(BF16)
        s1[j, 0] = far[:CHUNK // 2]
        s1[j, 1] = far[CHUNK // 2:]
        s1_copy(j, 0).start()
        s1_copy(j, 1).start()

        def near(q):
            part[slot, q] = quarter((x + jnp.where(q == 2, 3, q)) % 4)

        each(0, 3, near)

    def second(j):
        slot = j % HOLD
        mid = CHUNK // 2
        s1_wait(j, 0)
        s2[j, 0, :mid] = (part[slot, 1, :mid] + l1[j].astype(F32)).astype(BF16)
        s2[j, 0, mid:] = part[slot, 1, mid:].astype(BF16)
        s2_copy(j, 0).start()
        s1_wait(j, 1)
        s2[j, 1, :mid] = part[slot, 2, :mid].astype(BF16)
        s2[j, 1, mid:] = (part[slot, 2, mid:] + r1[j].astype(F32)).astype(BF16)
        s2_copy(j, 1).start()

    def s3_self(j, cc):
        return (2 * c + j // STRIPS == y) & (cc == c)

    def s3_copy(j, cc):
        return remote(
            s3.at[j, cc], r3.at[j % STRIPS, y], s3_s.at[j, cc], s3_r.at[j % STRIPS, y], dev(x, 2 * c + j // STRIPS, z, cc)
        )

    def third(j):
        slot = j % HOLD
        s2_wait(j, 0)
        s2_wait(j, 1)
        for cc in range(2):
            at = slice(cc * 2 * STRIP, (cc + 1) * 2 * STRIP)
            s3[j, cc] = part[slot, 0, at] + (l2[j, at].astype(F32) + r2[j, at].astype(F32))

            @pl.when(s3_self(j, cc))
            def _():
                pltpu.make_async_copy(s3.at[j, cc], r3.at[j % STRIPS, y], s3_r.at[j % STRIPS, y]).start()

            @pl.when(jnp.logical_not(s3_self(j, cc)))
            def _():
                s3_copy(j, cc).start()

    def z_send(n, zl, p):
        return remote(zs.at[n, zl, p], zr.at[n, z], z_s.at[n, zl, p], z_r.at[n, z], dev(x, y, 2 * p + zl, c))

    def fourth(n):
        for k in range(4):
            pltpu.make_async_copy(s3.at[0, 0], r3.at[n, k], s3_r.at[n, k]).wait()
        for zl in range(2):
            for h in range(2):
                at = slice(zl * STRIP + h * STRIP // 2, zl * STRIP + (h + 1) * STRIP // 2)
                total = (r3[n, 0, at] + r3[n, 1, at]) + (r3[n, 2, at] + r3[n, 3, at])
                zs[n, zl, 2 * h] = total[:, :128]
                zs[n, zl, 2 * h + 1] = total[:, 128:]

        def send(k):
            zl, p = k // 4, k % 4

            @pl.when(2 * p + zl == z)
            def _():
                pltpu.make_async_copy(zs.at[n, zl, p], zr.at[n, z], z_r.at[n, z]).start()

            @pl.when(2 * p + zl != z)
            def _():
                z_send(n, zl, p).start()

        each(0, 8, send)

    def a_copy(m, t):
        to = ((zhi + t) % 4) * 4 + x
        return remote(fb.at[m], ar.at[m, x, zhi], a_s.at[m, t], a_r.at[m, t], (to, me))

    def a_wait(m, t):
        remote(fb.at[m], ar.at[m, x, (zhi + 4 - t) % 4], a_s.at[m, t], a_r.at[m, t], sib).wait_recv()

    def b_copy(m, t):
        to = zhi * 4 + (x + t) % 4
        return remote(ar.at[m, x], ar.at[m, x], b_s.at[m, t], b_r.at[m, t], (to, me))

    def b_wait(m, t):
        src = (x + 4 - t) % 4
        remote(ar.at[m, src], ar.at[m, src], b_s.at[m, t], b_r.at[m, t], sib).wait_recv()

    def fifth(m):
        for e in range(2):
            n = 2 * m + e

            def wait(k):
                pltpu.make_async_copy(zs.at[0, 0, 0], zr.at[n, k], z_r.at[n, k]).wait()

            each(0, 8, wait)
        totals = []
        for e in range(2):
            total = zr[2 * m + e, 0]
            for k in range(1, 8):
                total = total + zr[2 * m + e, k]
            totals.append(total * FACTOR)
        both = jnp.concatenate(totals, axis=0).astype(BF16)
        fb[m] = both
        ar[m, x, zhi] = both
        each(1, 4, lambda t: a_copy(m, t).start())

    def sixth(m):
        each(1, 4, lambda t: a_wait(m, t))
        each(1, 4, lambda t: b_copy(m, t).start())

    first = STRIPS * (y % 2)

    def step(i):
        pl.when(i < CHUNKS)(lambda: matmul(i))
        pl.when((i >= 2) & (i < CHUNKS + 2))(lambda: second(i - 2))
        pl.when((i >= 4) & (i < CHUNKS + 4))(lambda: third(i - 4))
        n = i - 6 - first
        pl.when((n >= 0) & (n < STRIPS))(lambda: fourth(n))
        n = i - 8 - first
        pl.when((n >= 0) & (n < STRIPS) & (n % 2 == 1))(lambda: fifth(n // 2))
        n = i - 10 - first
        pl.when((n >= 0) & (n < STRIPS) & (n % 2 == 1))(lambda: sixth(n // 2))

        tasks = {
            0: [lambda: w_near(0, 0), lambda: w_near(1, 0), lambda: w_other(0, 0), lambda: w_other(0, 1), lambda: hidden_other(3)],
            1: [lambda: hidden_other(4), lambda: hidden_other(5), lambda: each(STRIPS, CHUNKS, lambda j: h_copy(j).start())],
            2: [lambda: w_near(0, 1), lambda: w_near(1, 1), lambda: delta(0)],
            3: [lambda: hidden_own(3), lambda: hidden_own(4), lambda: hidden_own(5)],
            4: [lambda: w_far(0), lambda: w_far(1), lambda: w_other(3, 0), lambda: w_other(1, 1)],
            6: [lambda: w_other(1, 0), lambda: w_other(3, 1)],
            7: [lambda: delta(1), lambda: w_other(2, 0), lambda: w_other(2, 1)],
            8: [lambda: delta(3)],
            9: [lambda: delta(2), gain_first],
            10: [finish],
            12: [gain_second],
        }
        for at, todo in tasks.items():
            def run(todo=todo):
                for task in todo:
                    task()

            pl.when(i == at)(run)

    each(0, CHUNKS + 10, step)

    gain_third()

    def place(m):
        each(1, 4, lambda t: b_wait(m, t))
        for xs in range(4):
            for p in range(4):
                both = ar[m, xs, p].astype(F32)
                lanes = slice(QUART * xs + 128 * (p % 2), QUART * xs + 128 * (p % 2) + 128)
                for e in range(2):
                    rows = ds((2 * m + e) * STRIP + STRIP // 2 * (p // 2), STRIP // 2, 8)
                    wg[rows, lanes] = both[e * STRIP // 2:(e + 1) * STRIP // 2]

    each(0, STRIPS // 2, place)

    def sent(t):
        gain_copy(t).wait_send()
        g1_copy(t).wait_send()
        g2_copy(t).wait_send()

    each(1, 16, sent)
    u_copy.wait_send()
    each(0, CHUNKS, lambda j: h_copy(j).wait_send())
    for way in range(2):
        for h in range(2):
            y_own(way, h).wait_send()
        y_pass(way).wait_send()
    for d in range(4):
        for h in range(2):
            z_half(d, h).wait_send()
            for k in range(2):
                c_half(d, h, k).wait_send()

    def sums_sent(j):
        for h in range(2):
            s1_copy(j, h).wait_send()
            s2_copy(j, h).wait_send()
            pl.when(jnp.logical_not(s3_self(j, h)))(lambda h=h: s3_copy(j, h).wait_send())

    each(0, CHUNKS, sums_sent)

    def z_sent(k):
        n, zl, p = k // 8, (k // 4) % 2, k % 4
        pl.when(2 * p + zl != z)(lambda: z_send(n, zl, p).wait_send())

    each(0, 8 * STRIPS, z_sent)

    def replicas_sent(m):
        def one(t):
            a_copy(m, t).wait_send()
            b_copy(m, t).wait_send()

        each(1, 4, one)

    each(0, STRIPS // 2, replicas_sent)


def local(inputs, gain, weight, upstream):
    vmem = pltpu.VMEM
    dma = pltpu.SemaphoreType.DMA
    anywhere = pl.BlockSpec(memory_space=pl.ANY)
    whole = pl.BlockSpec(memory_space=pltpu.VMEM)
    input_grad, weight_grad, gain_grad = pl.pallas_call(
        kernel,
        out_shape=(
            vmem((TOK, D), BF16),
            vmem((ROWS, COLS), F32),
            vmem((ROWS,), F32),
        ),
        in_specs=[anywhere, whole, anywhere, anywhere],
        out_specs=(whole, whole, whole),
        scratch_shapes=[
            vmem((TOK, D), BF16),
            vmem((D, COLS), BF16),
            vmem((TOK, D), F32),
            vmem((HALF, 2 * TOK), BF16),
            vmem((HALF, TOK), BF16),
            vmem((2 * TOK, COLS), BF16),
            vmem((TOK, 128), F32),
            vmem((TOK, 128), F32),
            vmem((1, PAD), F32),
            vmem((1, PAD), F32),
            vmem((16, 1, 512), F32),
            vmem((16, 1, 512), F32),
            vmem((16, 1, 512), F32),
            vmem((1, 512), F32),
            vmem((1, 512), F32),
            vmem((HOLD, 3, CHUNK, QUART), F32),
            vmem((CHUNKS, 2, CHUNK // 2, QUART), BF16),
            vmem((CHUNKS, CHUNK // 2, QUART), BF16),
            vmem((CHUNKS, CHUNK // 2, QUART), BF16),
            vmem((CHUNKS, 2, CHUNK, QUART), BF16),
            vmem((CHUNKS, CHUNK, QUART), BF16),
            vmem((CHUNKS, CHUNK, QUART), BF16),
            vmem((CHUNKS, 2, CHUNK // 2, QUART), F32),
            vmem((STRIPS, 4, CHUNK // 2, QUART), F32),
            vmem((STRIPS, 2, 4, STRIP // 2, 128), F32),
            vmem((STRIPS, 8, STRIP // 2, 128), F32),
            vmem((STRIPS // 2, STRIP, 128), BF16),
            vmem((STRIPS // 2, 4, 4, STRIP, 128), BF16),
            dma((8,)), dma, dma,
            dma((16,)), dma((16,)), dma((16,)), dma((16,)), dma((16,)), dma((16,)),
            dma, dma, dma((CHUNKS,)), dma((CHUNKS,)),
            dma((3, 2)), dma((3, 2)), dma((4, 2)), dma((4, 2)), dma((4, 2, 2)), dma((4, 2, 2)),
            dma((CHUNKS, 2)), dma((CHUNKS, 2)), dma((CHUNKS, 2)), dma((CHUNKS, 2)), dma((CHUNKS, 2)), dma((STRIPS, 4)),
            dma((STRIPS, 2, 4)), dma((STRIPS, 8)),
            dma((STRIPS // 2, 4)), dma((STRIPS // 2, 4)), dma((STRIPS // 2, 4)), dma((STRIPS // 2, 4)),
        ],
        compiler_params=pltpu.CompilerParams(
            collective_id=0, has_side_effects=True, vmem_limit_bytes=54 << 20
        ),
        name="backward",
    )(inputs, gain, weight, upstream)
    return input_grad, weight_grad, gain_grad


def solution(mesh):
    return jax.shard_map(
        local,
        mesh=mesh,
        in_specs=(
            P(("rep", "shard"), None),
            P("shard"),
            P("shard", None),
            P(("rep", "shard"), None),
        ),
        out_specs=(P(("rep", "shard"), None), P("shard", None), P("shard")),
        check_vma=False,
    )
```

time: 471 us -> 111 us (0.24)
  waiting for transfers between devices: 279 us -> 0 us
  blocking collectives: 134 us -> 0 us
  Pallas kernels: 0 us -> 105 us
  matrix products: 24.8 us -> 0 us
  other arithmetic: 16.8 us -> 0 us
  between operations: 14.5 us -> 0.64 us
    psum x1 -> x0, waiting for transfers between devices: 164 us -> none  [local(): weight_grad = lax.psum(shard_grad, 'rep') * factor]
    reduce_scatter x1 -> x0, waiting for transfers between devices: 114 us -> none  [local(): lax.psum_scatter(lax.dot_general(hidden, upstream, (((0,), (0,)), ((), ()...]
    pallas_call x0 -> x1, Pallas kernels: none -> 105 us  [local(): pl.pallas_call(kernel, out_shape=(vmem((TOK, D), BF16), vmem((ROWS, COLS)...]
    psum x1 -> x0, blocking collectives: 83.2 us -> none  [local(): gain_total = lax.psum(gain_part, ('rep', 'shard'))]
    unnamed x1 -> x0, blocking collectives: 50.3 us -> none
    dot_general x2 -> x0, matrix products: 24.8 us -> none  [the longest x1 13.1 us: local(): lax.dot_general(upstream, weight_piece, (((1,), (1,)), ((), ())), preferr...]
    convert_element_type x1 -> x0, other arithmetic: 10.3 us -> none  [local(): input_grad = (inverse * (scaled - normed * jnp.mean(scaled * normed, axis...]
  transfers between devices with their start and end apart: 3 -> 0, of which waited for: 2 -> 0; matrix products, arithmetic and copies ran while one was open for 9% -> 0% of each run, Pallas kernels for 0% -> 0%
where the time goes in v1:
time: 111 us; the launch traced here: 109 us
  Pallas kernels  105 us (95%)
  local copies, waits for them, and re-layouts  3.78 us (3%)
    pallas_call x1, Pallas kernels, local(): pl.pallas_call(kernel, out_shape=(vmem((TOK, D), BF16), vmem((ROWS, COLS)...  105 us
    unnamed x3, local copies, waits for them, and re-layouts  3.78 us

profile of v1, /device:TPU:8, one launch (start us, length us, event | category | flops | bytes accessed | tf_op | source)
XLA Modules:
  0.0 109.4 jit_solution(7701032748101974113)
XLA Ops:
  0.6 105.0 %backward.1 = (bf16[512,4608]{1,0:T(8,128)(2,1)S(1)}, f32[288,1024]{1,0:T(8,128)S(1)}, f32[288]{0:T(512)S(1)}) custom-call(bf16[512,4608]{1,0:T(8,128)(2,1)} %x_hbm.1, bf16[288]{0:T(512)(128)(2,1)} %gain.1, bf16[288,1024]{1,0:T(8,128)(2,1)} %w_hbm.1, bf16[512,1024]{1,0:T(8,128)(2,1)} %u_hbm.1), custom_call_target="tpu_custom_call" | custom-call | tf_op jit(solution)/shard_map/backward/pallas_call | solution.py:534
  105.6 2.2 %copy.10 = bf16[512,4608]{1,0:T(8,128)(2,1)} copy(bf16[512,4608]{1,0:T(8,128)(2,1)S(1)} %get-tuple-element.3) | data formatting | bytes 9437184
  107.8 0.6 copy.12
  108.4 1.0 copy.11

commit v2 on v1

--- a/solution.py
+++ b/solution.py
@@ -91,6 +91,67 @@
     each(1, 16, lambda t: hello((rep, (me + t) % 16)))
     each(1, 16, lambda t: hello(((rep + t) % 16, me)))
     each(1, 4, lambda t: hello((((zhi + t) % 4) * 4 + x, (y * 2 + 1 - zlo) * 2 + c)))
+    pl.semaphore_wait(barrier, 33)
+
+    def gain_copy(t):
+        return remote(win, gbuf.at[me], gb_s.at[t], gb_r.at[t], (rep, (me + t) % 16))
+
+    each(1, 16, lambda t: gain_copy(t).start())
+    gbuf[me] = win[...]
+    u_copy = remote(u_hbm, ups.at[own_tok, :], u_s, u_r, sib)
+    u_copy.start()
+
+    def w_half(d, zl, cc, h):
+        return ds(((((y + d) % 4) * 2 + zl) * 2 + cc) * ROWS + h * 144, 144, 16)
+
+    def y_own(way, h):
+        rows = w_half(0, zlo, c, h)
+        to = dev(x, (y + (1 if way == 0 else 3)) % 4, z, c)
+        return remote(wv.at[rows, :], wv.at[rows, :], wy_s.at[way, h], wy_r.at[way, h], to)
+
+    def y_pass(way):
+        rows = w_half(3 if way == 0 else 1, zlo, c, way)
+        to = dev(x, (y + (1 if way == 0 else 3)) % 4, z, c)
+        return remote(wv.at[rows, :], wv.at[rows, :], wy_s.at[2, way], wy_r.at[2, way], to)
+
+    def z_half(d, h):
+        rows = w_half(d, zlo, c, h)
+        return remote(wv.at[rows, :], wv.at[rows, :], wz_s.at[d, h], wz_r.at[d, h], up if h == 0 else down)
+
+    def c_half(d, h, k):
+        rows = w_half(d, zlo if k == 0 else 1 - zlo, c, h)
+        return remote(wv.at[rows, :], wv.at[rows, :], wc_s.at[d, h, k], wc_r.at[d, h, k], sib)
+
+    def arrive(rows, sem):
+        remote(wv.at[rows, :], wv.at[rows, :], wc_s.at[0, 0, 0], sem, sib).wait_recv()
+
+    def w_have(d, h):
+        z_half(d, h).start()
+        c_half(d, h, 0).start()
+
+    def w_near(h, k):
+        way = h if k == 0 else 1 - h
+        d = 3 if way == 0 else 1
+        arrive(w_half(d, zlo, c, h), wy_r.at[way, h])
+        if k == 0:
+            y_pass(way).start()
+        w_have(d, h)
+
+    def w_far(h):
+        arrive(w_half(2, zlo, c, h), wy_r.at[2, h])
+        w_have(2, h)
+
+    def w_other(d, h):
+        arrive(w_half(d, 1 - zlo, c, h), wz_r.at[d, h])
+        c_half(d, h, 1).start()
+
+    load_w.wait()
+    for way in (0, 1):
+        y_own(way, way).start()
+        w_have(0, way)
+    for way in (0, 1):
+        y_own(way, 1 - way).start()
+
     def norm_block(k):
         load_x(k).wait()
         rows = ds(k * 64, 64, 64)
@@ -104,67 +165,6 @@
 
     each(0, 8, norm_block)
 
-    pl.semaphore_wait(barrier, 33)
-
-    def gain_copy(t):
-        return remote(win, gbuf.at[me], gb_s.at[t], gb_r.at[t], (rep, (me + t) % 16))
-
-    each(1, 16, lambda t: gain_copy(t).start())
-    gbuf[me] = win[...]
-    u_copy = remote(u_hbm, ups.at[own_tok, :], u_s, u_r, sib)
-    u_copy.start()
-
-    def w_half(d, zl, cc, h):
-        return ds(((((y + d) % 4) * 2 + zl) * 2 + cc) * ROWS + h * 144, 144, 16)
-
-    def y_own(way, h):
-        rows = w_half(0, zlo, c, h)
-        to = dev(x, (y + (1 if way == 0 else 3)) % 4, z, c)
-        return remote(wv.at[rows, :], wv.at[rows, :], wy_s.at[way, h], wy_r.at[way, h], to)
-
-    def y_pass(way):
-        rows = w_half(3 if way == 0 else 1, zlo, c, way)
-        to = dev(x, (y + (1 if way == 0 else 3)) % 4, z, c)
-        return remote(wv.at[rows, :], wv.at[rows, :], wy_s.at[2, way], wy_r.at[2, way], to)
-
-    def z_half(d, h):
-        rows = w_half(d, zlo, c, h)
-        return remote(wv.at[rows, :], wv.at[rows, :], wz_s.at[d, h], wz_r.at[d, h], up if h == 0 else down)
-
-    def c_half(d, h, k):
-        rows = w_half(d, zlo if k == 0 else 1 - zlo, c, h)
-        return remote(wv.at[rows, :], wv.at[rows, :], wc_s.at[d, h, k], wc_r.at[d, h, k], sib)
-
-    def arrive(rows, sem):
-        remote(wv.at[rows, :], wv.at[rows, :], wc_s.at[0, 0, 0], sem, sib).wait_recv()
-
-    def w_have(d, h):
-        z_half(d, h).start()
-        c_half(d, h, 0).start()
-
-    def w_near(h, k):
-        way = h if k == 0 else 1 - h
-        d = 3 if way == 0 else 1
-        arrive(w_half(d, zlo, c, h), wy_r.at[way, h])
-        if k == 0:
-            y_pass(way).start()
-        w_have(d, h)
-
-    def w_far(h):
-        arrive(w_half(2, zlo, c, h), wy_r.at[2, h])
-        w_have(2, h)
-
-    def w_other(d, h):
-        arrive(w_half(d, 1 - zlo, c, h), wz_r.at[d, h])
-        c_half(d, h, 1).start()
-
-    load_w.wait()
-    for way in (0, 1):
-        y_own(way, way).start()
-        w_have(0, way)
-    for way in (0, 1):
-        y_own(way, 1 - way).start()
-
     def gain_wait(t):
         remote(win, gbuf.at[(me + 16 - t) % 16], gb_s.at[t], gb_r.at[t], sib).wait_recv()
 
@@ -208,64 +208,65 @@
     def hidden_own(j):
         hidden_block(j, c * HALF, ht, c * TOK)
 
-    each(0, 3, hidden_other)
-    each(0, STRIPS, lambda j: h_copy(j).start())
-    each(0, 3, hidden_own)
+    odd = y % 2
+    early, late = 3 * odd, 3 * (1 - odd)
+
+    def chunk_of(i):
+        return ((i // STRIPS + odd) % 2) * STRIPS + i % STRIPS
+
+    each(0, 3, lambda j: hidden_other(early + j))
+    each(0, STRIPS, lambda j: h_copy(chunk_of(j)).start())
+    each(0, 3, lambda j: hidden_own(early + j))
     load_u.wait()
     remote(u_hbm, ups.at[ds((1 - c) * TOK, TOK, TOK), :], u_s, u_r, sib).wait_recv()
 
     rd[...] = jnp.zeros_like(rd)
     gsum[...] = jnp.zeros_like(gsum)
 
-    def delta(d):
+    def projection(d):
         for h in range(2):
             for k in range(2):
                 arrive(w_half(d, zlo if k == 0 else 1 - zlo, 1 - c, h), wc_r.at[d, h, k])
 
-        def block(j):
-            at = ((y + d) % 4) * 1152 + j * SUB
-            feats = ds(at, SUB, 128)
-            sv[:, feats] = lax.dot_general(
-                ups[own_tok, :], wv[ds(at, SUB, 32), :], (((1,), (1,)), ((), ())), preferred_element_type=F32
-            )
-            scale = gfull[:, feats]
-
-            def tokens(k, col):
-                rows = ds(k * 64, 64, 64)
-                dl = sv[rows, feats]
-                nm = xv[rows, feats].astype(F32) * inv3(rows)
-                dn = dl * nm
-                sn = dn * scale
-                sv[rows, feats] = dl * scale
-                rd[rows, :] = rd[rows, :] + (sn[:, :128] + sn[:, 128:256] + sn[:, 256:])
-                return col + jnp.sum(dn.reshape(8, 8, SUB), axis=0)
-
-            col = lax.fori_loop(0, 8, tokens, jnp.zeros((8, SUB), F32))
-            gsum[:, feats] = jnp.sum(col, axis=0, keepdims=True)
-
-        each(0, 3, block)
-
-    def finish():
-        def mean(k):
+    def delta(b):
+        e = b // 3
+        d = jnp.where(e == 2, 3, jnp.where(e == 3, 2, e))
+        at = ((y + d) % 4) * 1152 + (b % 3) * SUB
+        feats = ds(at, SUB, 128)
+        sv[:, feats] = lax.dot_general(
+            ups[own_tok, :], wv[ds(at, SUB, 32), :], (((1,), (1,)), ((), ())), preferred_element_type=F32
+        )
+        scale = gfull[:, feats]
+
+        def tokens(k, col):
             rows = ds(k * 64, 64, 64)
-            m = jnp.sum(rd[rows, :], axis=-1, keepdims=True) * (1.0 / D)
-            rd[rows, :] = jnp.broadcast_to(m, (64, 128))
-
-        each(0, 8, mean)
-
+            dl = sv[rows, feats]
+            nm = xv[rows, feats].astype(F32) * inv3(rows)
+            dn = dl * nm
+            sn = dn * scale
+            sv[rows, feats] = dl * scale
+            rd[rows, :] = rd[rows, :] + (sn[:, :128] + sn[:, 128:256] + sn[:, 256:])
+            return col + jnp.sum(dn.reshape(8, 8, SUB), axis=0)
+
+        col = lax.fori_loop(0, 8, tokens, jnp.zeros((8, SUB), F32))
+        gsum[:, feats] = jnp.sum(col, axis=0, keepdims=True)
+
+    def finish(first, last):
         def block(j):
             rows = ds(j * 64, 64, 64)
+            m = jnp.sum(rd[rows, :], axis=-1, keepdims=True) * (1.0 / D)
+            m = jnp.broadcast_to(m, (64, 128))
+            m = jnp.concatenate([m, m, m], axis=1)
 
             def part_of(k):
                 feats = ds(k * SUB, SUB, 128)
                 iv = inv3(rows)
-                m = rd[rows, :]
                 nm = xv[rows, feats].astype(F32) * iv
-                ig[rows, feats] = (iv * (sv[rows, feats] - nm * jnp.concatenate([m, m, m], axis=1))).astype(BF16)
+                ig[rows, feats] = (iv * (sv[rows, feats] - nm * m)).astype(BF16)
 
             each(0, 12, part_of)
 
-        each(0, 8, block)
+        each(first, last, block)
 
     def gain_window(s):
         return ds(s * ROWS - (32 * s) % 128, 512, 128)
@@ -317,9 +318,9 @@
         remote(s2.at[j, h], (l2 if h == 0 else r2).at[j], s2_s.at[j, h], s2_r.at[j, h], left).wait_recv()
 
     def matmul(j):
-        h_wait(j)
+        h_wait(chunk_of(j))
         slot = j % HOLD
-        rows = ds(j * CHUNK, CHUNK, CHUNK)
+        rows = ds(chunk_of(j) * CHUNK, CHUNK, CHUNK)
 
         def quarter(q):
             return jnp.dot(ht[rows, :], ups[:, ds(q * QUART, QUART, 128)], preferred_element_type=F32)
@@ -347,12 +348,15 @@
         s2[j, 1, mid:] = (part[slot, 2, mid:] + r1[j].astype(F32)).astype(BF16)
         s2_copy(j, 1).start()
 
+    def s3_to(j):
+        return 2 * c + (j // STRIPS + odd) % 2
+
     def s3_self(j, cc):
-        return (2 * c + j // STRIPS == y) & (cc == c)
+        return (s3_to(j) == y) & (cc == c)
 
     def s3_copy(j, cc):
         return remote(
-            s3.at[j, cc], r3.at[j % STRIPS, y], s3_s.at[j, cc], s3_r.at[j % STRIPS, y], dev(x, 2 * c + j // STRIPS, z, cc)
+            s3.at[j, cc], r3.at[j % STRIPS, y], s3_s.at[j, cc], s3_r.at[j % STRIPS, y], dev(x, s3_to(j), z, cc)
         )
 
     def third(j):
@@ -435,43 +439,6 @@
         each(1, 4, lambda t: a_wait(m, t))
         each(1, 4, lambda t: b_copy(m, t).start())
 
-    first = STRIPS * (y % 2)
-
-    def step(i):
-        pl.when(i < CHUNKS)(lambda: matmul(i))
-        pl.when((i >= 2) & (i < CHUNKS + 2))(lambda: second(i - 2))
-        pl.when((i >= 4) & (i < CHUNKS + 4))(lambda: third(i - 4))
-        n = i - 6 - first
-        pl.when((n >= 0) & (n < STRIPS))(lambda: fourth(n))
-        n = i - 8 - first
-        pl.when((n >= 0) & (n < STRIPS) & (n % 2 == 1))(lambda: fifth(n // 2))
-        n = i - 10 - first
-        pl.when((n >= 0) & (n < STRIPS) & (n % 2 == 1))(lambda: sixth(n // 2))
-
-        tasks = {
-            0: [lambda: w_near(0, 0), lambda: w_near(1, 0), lambda: w_other(0, 0), lambda: w_other(0, 1), lambda: hidden_other(3)],
-            1: [lambda: hidden_other(4), lambda: hidden_other(5), lambda: each(STRIPS, CHUNKS, lambda j: h_copy(j).start())],
-            2: [lambda: w_near(0, 1), lambda: w_near(1, 1), lambda: delta(0)],
-            3: [lambda: hidden_own(3), lambda: hidden_own(4), lambda: hidden_own(5)],
-            4: [lambda: w_far(0), lambda: w_far(1), lambda: w_other(3, 0), lambda: w_other(1, 1)],
-            6: [lambda: w_other(1, 0), lambda: w_other(3, 1)],
-            7: [lambda: delta(1), lambda: w_other(2, 0), lambda: w_other(2, 1)],
-            8: [lambda: delta(3)],
-            9: [lambda: delta(2), gain_first],
-            10: [finish],
-            12: [gain_second],
-        }
-        for at, todo in tasks.items():
-            def run(todo=todo):
-                for task in todo:
-                    task()
-
-            pl.when(i == at)(run)
-
-    each(0, CHUNKS + 10, step)
-
-    gain_third()
-
     def place(m):
         each(1, 4, lambda t: b_wait(m, t))
         for xs in range(4):
@@ -482,7 +449,50 @@
                     rows = ds((2 * m + e) * STRIP + STRIP // 2 * (p // 2), STRIP // 2, 8)
                     wg[rows, lanes] = both[e * STRIP // 2:(e + 1) * STRIP // 2]
 
-    each(0, STRIPS // 2, place)
+    def step(i):
+        pl.when(i < CHUNKS)(lambda: matmul(i))
+        pl.when((i >= 2) & (i < CHUNKS + 2))(lambda: second(i - 2))
+        pl.when((i >= 4) & (i < CHUNKS + 4))(lambda: third(i - 4))
+        n = i - 6 - STRIPS
+        pl.when((n >= 0) & (n < STRIPS))(lambda: fourth(n))
+        n = i - 8 - STRIPS
+        pl.when((n >= 0) & (n < STRIPS) & (n % 2 == 1))(lambda: fifth(n // 2))
+        n = i - 10 - STRIPS
+        pl.when((n >= 0) & (n < STRIPS) & (n % 2 == 1))(lambda: sixth(n // 2))
+
+        tasks = {
+            0: [lambda: each(0, 2, lambda j: hidden_other(late + j))],
+            1: [lambda: hidden_other(late + 2), lambda: each(STRIPS, CHUNKS, lambda j: h_copy(chunk_of(j)).start()),
+                lambda: w_near(0, 0), lambda: w_near(1, 0), lambda: w_other(0, 0), lambda: w_other(0, 1),
+                lambda: hidden_own(late)],
+            2: [lambda: hidden_own(late + 1)],
+            3: [lambda: w_near(0, 1), lambda: w_near(1, 1), lambda: hidden_own(late + 2)],
+            4: [lambda: projection(0)],
+            5: [lambda: w_far(0), lambda: w_far(1), lambda: w_other(3, 0), lambda: w_other(1, 1)],
+            7: [lambda: w_other(1, 0), lambda: w_other(3, 1)],
+            8: [lambda: projection(1)],
+            9: [lambda: w_other(2, 0), lambda: w_other(2, 1)],
+            11: [lambda: projection(3)],
+            14: [lambda: projection(2)],
+            17: [gain_first],
+            19: [gain_second],
+            20: [lambda: place(0)],
+            21: [lambda: place(1)],
+        }
+        for at, todo in tasks.items():
+            def run(todo=todo):
+                for task in todo:
+                    task()
+
+            pl.when(i == at)(run)
+
+        pl.when(((i >= 4) & (i < 7)) | ((i >= 8) & (i < 17)))(lambda: delta(jnp.where(i < 7, i - 4, i - 5)))
+        pl.when((i >= 17) & (i < 21))(lambda: finish(2 * (i - 17), 2 * (i - 17) + 2))
+
+    each(0, CHUNKS + 10, step)
+
+    gain_third()
+    place(2)
 
     def sent(t):
         gain_copy(t).wait_send()
@@ -524,6 +534,15 @@
         each(1, 4, one)
 
     each(0, STRIPS // 2, replicas_sent)
+
+
+def hand_out(ig, wg, gg, ig_hbm, wg_hbm, gg_hbm, sems):
+    copies = [pltpu.make_async_copy(ig.at[pl.ds(k * 64, 64)], ig_hbm.at[pl.ds(k * 64, 64)], sems.at[k]) for k in range(8)]
+    copies += [pltpu.make_async_copy(wg, wg_hbm, sems.at[8]), pltpu.make_async_copy(gg, gg_hbm, sems.at[9])]
+    for copy in copies:
+        copy.start()
+    for copy in copies:
+        copy.wait()
 
 
 def local(inputs, gain, weight, upstream):
@@ -582,7 +601,16 @@
         ),
         name="backward",
     )(inputs, gain, weight, upstream)
-    return input_grad, weight_grad, gain_grad
+    held = [pltpu.with_memory_space_constraint(a, pltpu.VMEM) for a in (input_grad, weight_grad, gain_grad)]
+    return pl.pallas_call(
+        hand_out,
+        out_shape=tuple(jax.ShapeDtypeStruct(a.shape, a.dtype) for a in held),
+        in_specs=[whole] * 3,
+        out_specs=(anywhere,) * 3,
+        scratch_shapes=[dma((10,))],
+        compiler_params=pltpu.CompilerParams(vmem_limit_bytes=1 << 20),
+        name="hand_out",
+    )(*held)
 
 
 def solution(mesh):

time: 111 us -> 93.9 us (0.85)
  Pallas kernels: 105 us -> 92.4 us
  local copies, waits for them, and re-layouts: 3.78 us -> 0 us
    pallas_call x1, Pallas kernels: 105 us -> 89.8 us  [local(): pl.pallas_call(kernel, out_shape=(vmem((TOK, D), BF16), vmem((ROWS, COLS)...]
    unnamed x3 -> x0, local copies, waits for them, and re-layouts: 3.78 us -> none
    pallas_call x0 -> x1, Pallas kernels: none -> 2.66 us  [local(): pl.pallas_call(hand_out, out_shape=tuple((jax.ShapeDtypeStruct(a.shape, a...]
where the time goes in v2:
time: 93.9 us; the launch traced here: 93.1 us
  Pallas kernels  92.4 us (98%)
    pallas_call x1, Pallas kernels, local(): pl.pallas_call(kernel, out_shape=(vmem((TOK, D), BF16), vmem((ROWS, COLS)...  89.8 us
    pallas_call x1, Pallas kernels, local(): pl.pallas_call(hand_out, out_shape=tuple((jax.ShapeDtypeStruct(a.shape, a...  2.66 us

profile of v2, /device:TPU:8, one launch (start us, length us, event | category | flops | bytes accessed | tf_op | source)
XLA Modules:
  0.0 93.1 jit_solution(14854377608396742321)
XLA Ops:
  0.6 89.8 %backward.1 = (bf16[512,4608]{1,0:T(8,128)(2,1)S(1)}, f32[288,1024]{1,0:T(8,128)S(1)}, f32[288]{0:T(512)S(1)}) custom-call(bf16[512,4608]{1,0:T(8,128)(2,1)} %x_hbm.1, bf16[288]{0:T(512)(128)(2,1)} %gain.1, bf16[288,1024]{1,0:T(8,128)(2,1)} %w_hbm.1, bf16[512,1024]{1,0:T(8,128)(2,1)} %u_hbm.1), custom_call_target="tpu_custom_call" | custom-call | tf_op jit(solution)/shard_map/backward/pallas_call | solution.py:553
  90.4 2.7 %hand_out.1 = (bf16[512,4608]{1,0:T(8,128)(2,1)}, f32[288,1024]{1,0:T(8,128)}, f32[288]{0:T(512)}) custom-call(bf16[512,4608]{1,0:T(8,128)(2,1)S(1)} %get-tuple-element.6.ig, f32[288,1024]{1,0:T(8,128)S(1)} %get-tuple-element.7.wg, f32[288]{0:T(512)S(1)} %get-tuple-element.8.gg), custom_call_target="tpu_custom_call" | custom-call | tf_op jit(solution)/shard_map/hand_out/pallas_call | solution.py:605

commit v3 on v2

--- a/solution.py
+++ b/solution.py
@@ -45,11 +45,11 @@
 
 
 def kernel(
-    x_hbm, gain, w_hbm, u_hbm,
+    x_hbm, gain_hbm, w_hbm, u_hbm,
     ig, wg, gg,
-    xv, wv, sv, ht, hs, ups, inv, rd, gfull, gsum, gbuf, gone, gtwo, gmine, win,
+    xv, wv, sv, ht, hs, ups, inv, rd, gfull, gsum, gbuf, gone, gtwo, gmine, gpart, win, gain,
     part, s1, l1, r1, s2, l2, r2, s3, r3, zs, zr, fb, ar,
-    ld_x, ld_u, ld_w,
+    ld_g, ld_x, ld_u, ld_w,
     gb_s, gb_r, g1_s, g1_r, g2_s, g2_r,
     u_s, u_r, h_s, h_r,
     wy_s, wy_r, wz_s, wz_r, wc_s, wc_r,
@@ -68,8 +68,23 @@
     right, left = dev((x + 1) % 4, y, z, c), dev((x + 3) % 4, y, z, c)
     up, down = dev(x, y, (z + 1) % 8, c), dev(x, y, (z + 7) % 8, c)
 
-    row = jnp.concatenate([gain[...].astype(F32).reshape(1, ROWS), jnp.zeros((1, 512 - ROWS), F32)], axis=1)
-    win[...] = pltpu.roll(jnp.broadcast_to(row, (8, 512)), (32 * me) % 128, 1)[:1]
+    barrier = pltpu.get_barrier_semaphore()
+
+    def hello(device):
+        pl.semaphore_signal(barrier, inc=1, device_id=device, device_id_type=MESH)
+
+    each(1, 16, lambda t: hello((rep, (me + t) % 16)))
+
+    def hello_far(t):
+        far = ((zhi + t) % 4) * 4 + x
+        hello((far, me))
+        hello((far, (y * 2 + 1 - zlo) * 2 + c))
+        hello((zhi * 4 + (x + t) % 4, me))
+
+    each(1, 4, hello_far)
+
+    load_g = pltpu.make_async_copy(gain_hbm, gain, ld_g)
+    load_g.start()
 
     def load_x(k):
         rows = ds(k * 64, 64, 64)
@@ -83,15 +98,11 @@
     load_w = pltpu.make_async_copy(w_hbm, wv.at[own_rows, :], ld_w)
     load_w.start()
 
-    barrier = pltpu.get_barrier_semaphore()
-
-    def hello(device):
-        pl.semaphore_signal(barrier, inc=1, device_id=device, device_id_type=MESH)
-
-    each(1, 16, lambda t: hello((rep, (me + t) % 16)))
-    each(1, 16, lambda t: hello(((rep + t) % 16, me)))
-    each(1, 4, lambda t: hello((((zhi + t) % 4) * 4 + x, (y * 2 + 1 - zlo) * 2 + c)))
-    pl.semaphore_wait(barrier, 33)
+    load_g.wait()
+    row = jnp.concatenate([gain[...].astype(F32).reshape(1, ROWS), jnp.zeros((1, 512 - ROWS), F32)], axis=1)
+    win[...] = pltpu.roll(jnp.broadcast_to(row, (8, 512)), (32 * me) % 128, 1)[:1]
+
+    pl.semaphore_wait(barrier, 24)
 
     def gain_copy(t):
         return remote(win, gbuf.at[me], gb_s.at[t], gb_r.at[t], (rep, (me + t) % 16))
@@ -279,10 +290,16 @@
         remote(gmine, gone.at[(me + 16 - t) % 16], g1_s.at[t], g1_r.at[t], sib).wait_recv()
 
     def g2_copy(t):
-        return remote(gmine, gtwo.at[rep], g2_s.at[t], g2_r.at[t], ((rep + t) % 16, me))
+        return remote(gmine, gtwo.at[zhi], g2_s.at[t], g2_r.at[t], (((zhi + t) % 4) * 4 + x, me))
 
     def g2_wait(t):
-        remote(gmine, gtwo.at[(rep + 16 - t) % 16], g2_s.at[t], g2_r.at[t], sib).wait_recv()
+        remote(gmine, gtwo.at[(zhi + 4 - t) % 4], g2_s.at[t], g2_r.at[t], sib).wait_recv()
+
+    def g3_copy(t):
+        return remote(gpart, gtwo.at[4 + x], g2_s.at[4 + t], g2_r.at[4 + t], (zhi * 4 + (x + t) % 4, me))
+
+    def g3_wait(t):
+        remote(gpart, gtwo.at[4 + (x + 4 - t) % 4], g2_s.at[4 + t], g2_r.at[4 + t], sib).wait_recv()
 
     def gain_first():
         each(1, 16, lambda t: g1_copy(t).start())
@@ -294,14 +311,19 @@
         for s in range(1, 16):
             total = total + gone[s]
         gmine[...] = total
-        gtwo[rep] = total
-        each(1, 16, lambda t: g2_copy(t).start())
+        gtwo[zhi] = total
+        each(1, 4, lambda t: g2_copy(t).start())
 
     def gain_third():
-        each(1, 16, g2_wait)
-        total = gtwo[0]
-        for s in range(1, 16):
-            total = total + gtwo[s]
+        each(1, 4, g2_wait)
+        total = (gtwo[0] + gtwo[1]) + (gtwo[2] + gtwo[3])
+        gpart[...] = total
+        gtwo[4 + x] = total
+        each(1, 4, lambda t: g3_copy(t).start())
+
+    def gain_last():
+        each(1, 4, g3_wait)
+        total = (gtwo[4] + gtwo[5]) + (gtwo[6] + gtwo[7])
         total = jnp.broadcast_to(total * FACTOR, (8, 512))
         gg[...] = pltpu.roll(total, (512 - (32 * me) % 128) % 512, 1)[0, :ROWS]
 
@@ -466,17 +488,16 @@
                 lambda: w_near(0, 0), lambda: w_near(1, 0), lambda: w_other(0, 0), lambda: w_other(0, 1),
                 lambda: hidden_own(late)],
             2: [lambda: hidden_own(late + 1)],
-            3: [lambda: w_near(0, 1), lambda: w_near(1, 1), lambda: hidden_own(late + 2)],
-            4: [lambda: projection(0)],
-            5: [lambda: w_far(0), lambda: w_far(1), lambda: w_other(3, 0), lambda: w_other(1, 1)],
-            7: [lambda: w_other(1, 0), lambda: w_other(3, 1)],
-            8: [lambda: projection(1)],
-            9: [lambda: w_other(2, 0), lambda: w_other(2, 1)],
-            11: [lambda: projection(3)],
-            14: [lambda: projection(2)],
-            17: [gain_first],
-            19: [gain_second],
-            20: [lambda: place(0)],
+            3: [lambda: hidden_own(late + 2)],
+            4: [lambda: w_near(0, 1), lambda: w_near(1, 1), lambda: projection(0)],
+            6: [lambda: w_far(0), lambda: w_far(1), lambda: w_other(3, 0), lambda: w_other(1, 1)],
+            8: [lambda: w_other(1, 0), lambda: w_other(3, 1)],
+            9: [lambda: projection(1)],
+            10: [lambda: w_other(2, 0), lambda: w_other(2, 1), lambda: projection(3)],
+            12: [lambda: projection(2)],
+            15: [gain_first],
+            17: [gain_second],
+            20: [gain_third, lambda: place(0)],
             21: [lambda: place(1)],
         }
         for at, todo in tasks.items():
@@ -486,18 +507,17 @@
 
             pl.when(i == at)(run)
 
-        pl.when(((i >= 4) & (i < 7)) | ((i >= 8) & (i < 17)))(lambda: delta(jnp.where(i < 7, i - 4, i - 5)))
-        pl.when((i >= 17) & (i < 21))(lambda: finish(2 * (i - 17), 2 * (i - 17) + 2))
+        pl.when(((i >= 4) & (i < 7)) | ((i >= 9) & (i < 15)))(
+            lambda: delta(jnp.where(i < 7, i - 4, jnp.where(i < 12, 2 * i - 15, i - 3)))
+        )
+        pl.when((i >= 9) & (i < 12))(lambda: delta(2 * i - 14))
+        pl.when((i >= 16) & (i < 20))(lambda: finish(2 * (i - 16), 2 * (i - 16) + 2))
 
     each(0, CHUNKS + 10, step)
-
-    gain_third()
-    place(2)
 
     def sent(t):
         gain_copy(t).wait_send()
         g1_copy(t).wait_send()
-        g2_copy(t).wait_send()
 
     each(1, 16, sent)
     u_copy.wait_send()
@@ -526,6 +546,15 @@
 
     each(0, 8 * STRIPS, z_sent)
 
+    gain_last()
+    place(2)
+
+    def gains_sent(t):
+        g2_copy(t).wait_send()
+        g3_copy(t).wait_send()
+
+    each(1, 4, gains_sent)
+
     def replicas_sent(m):
         def one(t):
             a_copy(m, t).wait_send()
@@ -557,7 +586,7 @@
             vmem((ROWS, COLS), F32),
             vmem((ROWS,), F32),
         ),
-        in_specs=[anywhere, whole, anywhere, anywhere],
+        in_specs=[anywhere] * 4,
         out_specs=(whole, whole, whole),
         scratch_shapes=[
             vmem((TOK, D), BF16),
@@ -572,9 +601,11 @@
             vmem((1, PAD), F32),
             vmem((16, 1, 512), F32),
             vmem((16, 1, 512), F32),
-            vmem((16, 1, 512), F32),
+            vmem((8, 1, 512), F32),
             vmem((1, 512), F32),
             vmem((1, 512), F32),
+            vmem((1, 512), F32),
+            vmem((ROWS,), BF16),
             vmem((HOLD, 3, CHUNK, QUART), F32),
             vmem((CHUNKS, 2, CHUNK // 2, QUART), BF16),
             vmem((CHUNKS, CHUNK // 2, QUART), BF16),
@@ -588,8 +619,8 @@
             vmem((STRIPS, 8, STRIP // 2, 128), F32),
             vmem((STRIPS // 2, STRIP, 128), BF16),
             vmem((STRIPS // 2, 4, 4, STRIP, 128), BF16),
-            dma((8,)), dma, dma,
-            dma((16,)), dma((16,)), dma((16,)), dma((16,)), dma((16,)), dma((16,)),
+            dma, dma((8,)), dma, dma,
+            dma((16,)), dma((16,)), dma((16,)), dma((16,)), dma((8,)), dma((8,)),
             dma, dma, dma((CHUNKS,)), dma((CHUNKS,)),
             dma((3, 2)), dma((3, 2)), dma((4, 2)), dma((4, 2)), dma((4, 2, 2)), dma((4, 2, 2)),
             dma((CHUNKS, 2)), dma((CHUNKS, 2)), dma((CHUNKS, 2)), dma((CHUNKS, 2)), dma((CHUNKS, 2)), dma((STRIPS, 4)),

time: 93.9 us -> 90.7 us (0.966)
  Pallas kernels: 92.4 us -> 89.1 us
    pallas_call x1, Pallas kernels: 89.8 us -> 86.4 us  [local(): pl.pallas_call(kernel, out_shape=(vmem((TOK, D), BF16), vmem((ROWS, COLS)...]
where the time goes in v3:
time: 90.7 us; the launch traced here: 89.7 us
  Pallas kernels  89.1 us (98%)
    pallas_call x1, Pallas kernels, local(): pl.pallas_call(kernel, out_shape=(vmem((TOK, D), BF16), vmem((ROWS, COLS)...  86.4 us
    pallas_call x1, Pallas kernels, local(): pl.pallas_call(hand_out, out_shape=tuple((jax.ShapeDtypeStruct(a.shape, a...  2.66 us

profile of v3, /device:TPU:8, one launch (start us, length us, event | category | flops | bytes accessed | tf_op | source)
XLA Modules:
  0.0 89.7 jit_solution(5194484061766589154)
XLA Ops:
  0.6 86.4 %backward.1 = (bf16[512,4608]{1,0:T(8,128)(2,1)S(1)}, f32[288,1024]{1,0:T(8,128)S(1)}, f32[288]{0:T(512)S(1)}) custom-call(bf16[512,4608]{1,0:T(8,128)(2,1)} %x_hbm.1, bf16[288]{0:T(512)(128)(2,1)} %gain_hbm.1, bf16[288,1024]{1,0:T(8,128)(2,1)} %w_hbm.1, bf16[512,1024]{1,0:T(8,128)(2,1)} %u_hbm.1), custom_call_target="tpu_custom_call" | custom-call | tf_op jit(solution)/shard_map/backward/pallas_call | solution.py:582
  87.1 2.7 %hand_out.1 = (bf16[512,4608]{1,0:T(8,128)(2,1)}, f32[288,1024]{1,0:T(8,128)}, f32[288]{0:T(512)}) custom-call(bf16[512,4608]{1,0:T(8,128)(2,1)S(1)} %get-tuple-element.6.ig, f32[288,1024]{1,0:T(8,128)S(1)} %get-tuple-element.7.wg, f32[288]{0:T(512)S(1)} %get-tuple-element.8.gg), custom_call_target="tpu_custom_call" | custom-call | tf_op jit(solution)/shard_map/hand_out/pallas_call | solution.py:636

commit v4 on v3

--- a/solution.py
+++ b/solution.py
@@ -483,13 +483,12 @@
         pl.when((n >= 0) & (n < STRIPS) & (n % 2 == 1))(lambda: sixth(n // 2))
 
         tasks = {
-            0: [lambda: each(0, 2, lambda j: hidden_other(late + j))],
-            1: [lambda: hidden_other(late + 2), lambda: each(STRIPS, CHUNKS, lambda j: h_copy(chunk_of(j)).start()),
-                lambda: w_near(0, 0), lambda: w_near(1, 0), lambda: w_other(0, 0), lambda: w_other(0, 1),
-                lambda: hidden_own(late)],
-            2: [lambda: hidden_own(late + 1)],
-            3: [lambda: hidden_own(late + 2)],
-            4: [lambda: w_near(0, 1), lambda: w_near(1, 1), lambda: projection(0)],
+            1: [lambda: w_near(0, 0), lambda: w_near(1, 0)],
+            2: [lambda: hidden_other(late), lambda: w_other(0, 0), lambda: w_other(0, 1)],
+            3: [lambda: hidden_other(late + 1), lambda: hidden_other(late + 2),
+                lambda: each(STRIPS, CHUNKS, lambda j: h_copy(chunk_of(j)).start())],
+            4: [lambda: hidden_own(late), lambda: w_near(0, 1), lambda: w_near(1, 1), lambda: projection(0)],
+            5: [lambda: hidden_own(late + 1), lambda: hidden_own(late + 2)],
             6: [lambda: w_far(0), lambda: w_far(1), lambda: w_other(3, 0), lambda: w_other(1, 1)],
             8: [lambda: w_other(1, 0), lambda: w_other(3, 1)],
             9: [lambda: projection(1)],
@@ -507,8 +506,8 @@
 
             pl.when(i == at)(run)
 
-        pl.when(((i >= 4) & (i < 7)) | ((i >= 9) & (i < 15)))(
-            lambda: delta(jnp.where(i < 7, i - 4, jnp.where(i < 12, 2 * i - 15, i - 3)))
+        pl.when((i >= 6) & (i < 15))(
+            lambda: delta(jnp.where(i < 9, i - 6, jnp.where(i < 12, 2 * i - 15, i - 3)))
         )
         pl.when((i >= 9) & (i < 12))(lambda: delta(2 * i - 14))
         pl.when((i >= 16) & (i < 20))(lambda: finish(2 * (i - 16), 2 * (i - 16) + 2))

time: 90.7 us -> 88.1 us (0.971)
  Pallas kernels: 89.1 us -> 86.5 us
    pallas_call x1, Pallas kernels: 86.4 us -> 83.9 us  [local(): pl.pallas_call(kernel, out_shape=(vmem((TOK, D), BF16), vmem((ROWS, COLS)...]
where the time goes in v4:
time: 88.1 us; the launch traced here: 87.2 us
  Pallas kernels  86.5 us (98%)
    pallas_call x1, Pallas kernels, local(): pl.pallas_call(kernel, out_shape=(vmem((TOK, D), BF16), vmem((ROWS, COLS)...  83.9 us
    pallas_call x1, Pallas kernels, local(): pl.pallas_call(hand_out, out_shape=tuple((jax.ShapeDtypeStruct(a.shape, a...  2.66 us

profile of v4, /device:TPU:8, one launch (start us, length us, event | category | flops | bytes accessed | tf_op | source)
XLA Modules:
  0.0 87.2 jit_solution(1599937006256688266)
XLA Ops:
  0.6 83.9 %backward.1 = (bf16[512,4608]{1,0:T(8,128)(2,1)S(1)}, f32[288,1024]{1,0:T(8,128)S(1)}, f32[288]{0:T(512)S(1)}) custom-call(bf16[512,4608]{1,0:T(8,128)(2,1)} %x_hbm.1, bf16[288]{0:T(512)(128)(2,1)} %gain_hbm.1, bf16[288,1024]{1,0:T(8,128)(2,1)} %w_hbm.1, bf16[512,1024]{1,0:T(8,128)(2,1)} %u_hbm.1), custom_call_target="tpu_custom_call" | custom-call | tf_op jit(solution)/shard_map/backward/pallas_call | solution.py:581
  84.5 2.7 %hand_out.1 = (bf16[512,4608]{1,0:T(8,128)(2,1)}, f32[288,1024]{1,0:T(8,128)}, f32[288]{0:T(512)}) custom-call(bf16[512,4608]{1,0:T(8,128)(2,1)S(1)} %get-tuple-element.6.ig, f32[288,1024]{1,0:T(8,128)S(1)} %get-tuple-element.7.wg, f32[288]{0:T(512)S(1)} %get-tuple-element.8.gg), custom_call_target="tpu_custom_call" | custom-call | tf_op jit(solution)/shard_map/hand_out/pallas_call | solution.py:635
